TPU v7x, 32 devices: a whole 2x2x4 slice. The times are simulated.
32 devices in a mesh: grp: 2 (over x), rad: 8 (over z, y), chan: 2 (over core).
Axes of the slice: x: 2, y: 2, z: 4, core: 2. Of those that a mesh axis runs over, the one named last changes fastest.
Arguments:
- wave: bfloat16 [64, 2, 240, 1024], P('chan', None, 'rad', 'grp'), parts along dimension 3, may hold values from -6 to 6
- tile_elems: int32 [16], P(('grp', 'rad')), parts along dimension 0, may hold values from 1 to 2, 12 in all
- element_width: float32 [24], P('grp'), parts along dimension 0, may hold values from 0.7 to 1.4
- element_kinetic: float32 [16, 16], replicated, may hold values from -0.2 to 2, as said below
- radial_two: float32 [512, 512], replicated, may hold values from -1 to 4, as said below
- angular: float32 [2, 64, 64], replicated, may hold values from -24 to 24
- channel_table: int32 [64, 2], replicated, may hold values from 0 to 11, as said below
Outputs:
- evolved: float32 [64, 2, 240, 1024], P('chan', None, 'rad', 'grp'), parts along dimension 3
There are 2 independent parts, one for each index of `grp`. A program takes and returns all parts, laid end to end along the dimension named above; an argument that names none is the same for every part. Nothing has to cross between parts.
Inputs may be any that keep to these rules, and one draw needn't show every extreme that they name: `tile_elems`: the counts of one part sum to 12; some tile holds exactly 2 elements. `channel_table`: each row is a pair (l1, l2) of angular momenta; no two rows are equal; the pair (11, 11) is present. `element_kinetic`: A symmetric matrix. `radial_two`: A symmetric matrix.
All inputs are finite; a program needn't handle non-finite values. No bound on the sum of `tile_elems` on one device may be relied on, other than what follows from the above.
Results may differ from a plain program's by a relative error of at most 0.0003.
Values may be sent and summed in bfloat16 or wider, within the bound.
A program may use at most 64 MiB of HBM per device.

v0:
```python
import jax
import jax.numpy as jnp
from jax import lax
from jax.sharding import PartitionSpec as P

LAM = 2
PTS = 15


highest = lax.Precision.HIGHEST
charge = 2.0
inner_radius = 4.0
radial_step = 0.1
time_step = 0.1


def carried_in(part, axis, combine, identity):
    place = lax.axis_index(axis)
    gathered = lax.all_gather(part, axis)
    state = jnp.zeros_like(part) + jnp.asarray(identity, part.dtype)

    def one(hop, state):
        return combine(state, lax.dynamic_index_in_dim(gathered, hop, 0, False))

    return lax.fori_loop(0, place, one, state)


def from_behind(value, axis, steps):
    count = lax.axis_size(axis)
    leading, last = (max(0, -steps), min(count, count - steps))
    return lax.ppermute(value, axis, [(source, source + steps) for source in range(leading, last)])


def as_sent(shard):
    return jax.tree.map(lambda a: a.astype(jnp.bfloat16) if a.dtype == jnp.float32 else a, shard)


def node_fractions():
    points = jnp.arange(PTS, dtype=jnp.float32)
    return 0.5 * (1.0 - jnp.cos(jnp.pi * points / PTS))


def allowed_pairs(orbital_a, orbital_b, multipole):
    lower_bound = jnp.abs(orbital_a[:, None] - orbital_b[None, :])
    upper_bound = orbital_a[:, None] + orbital_b[None, :]
    return (
        (lower_bound <= multipole)
        & (multipole <= upper_bound)
        & ((upper_bound + multipole) % 2 == 0)
    )


def couplings(angular, channel_table):
    orbital_first = channel_table[:, 0]
    orbital_second = channel_table[:, 1]
    matrices = []
    for multipole in range(LAM):
        selected = allowed_pairs(orbital_first, orbital_first, multipole) & allowed_pairs(
            orbital_second, orbital_second, multipole
        )
        symmetric = 0.5 * (angular[multipole] + angular[multipole].T)
        matrices.append(jnp.where(selected, symmetric, 0.0))
    return jnp.stack(matrices)


def radial_weights(r_one, r_two):
    nearer = jnp.minimum(r_one[..., None], r_two)
    farther = jnp.maximum(r_one[..., None], r_two)
    return jnp.stack([nearer**multipole / farther ** (multipole + 1) for multipole in range(LAM)])


def diagonal_terms(table_rows, r_one, r_two):
    orbital_first = table_rows[:, 0].astype(jnp.float32)
    orbital_second = table_rows[:, 1].astype(jnp.float32)
    centri_first = 0.5 * orbital_first * (orbital_first + 1.0)
    centri_second = 0.5 * orbital_second * (orbital_second + 1.0)
    inv_one = 1.0 / r_one
    inv_two = 1.0 / r_two
    angular_part = centri_first[:, None, None, None] * (inv_one * inv_one)[
        None, :, :, None
    ] + centri_second[:, None, None, None] * (inv_two * inv_two)
    return angular_part - charge * (inv_one[None, :, :, None] + inv_two)


def propagate(field, apply_ham):
    taylor_term = field
    running = field
    applied = apply_ham(taylor_term)
    taylor_term = time_step / 1 * jnp.stack([applied[:, 1], -applied[:, 0]], axis=1)
    running = running + taylor_term
    return running


def combine_counts(earlier, later):
    return earlier + later


def slot_geometry(element_width, first_elem, count, padding):
    total_elems = element_width.shape[0]
    starts_all = jnp.concatenate([jnp.zeros((1,), jnp.float32), jnp.cumsum(element_width)])[
        :total_elems
    ]
    widths_ext = jnp.concatenate([element_width, jnp.ones((padding,), jnp.float32)])
    starts_ext = jnp.concatenate([starts_all, jnp.zeros((padding,), jnp.float32)])
    slot_width = lax.dynamic_slice_in_dim(widths_ext, first_elem, count)
    slot_start = lax.dynamic_slice_in_dim(starts_ext, first_elem, count)
    r_one = inner_radius + slot_start[:, None] + slot_width[:, None] * node_fractions()[None, :]
    return (slot_width, r_one)


def per_device(
    wave, tile_elems, element_width, element_kinetic, radial_two, angular, channel_table
):
    local_chan, parts_two, local_rows, width_two = wave.shape
    slot_count = local_rows // PTS
    tile_count = tile_elems[0]
    tile_offset = carried_in(tile_count, "rad", combine_counts, jnp.zeros((), jnp.int32))
    tile_offset = tile_offset.astype(jnp.int32)
    r_two = inner_radius + radial_step * jnp.arange(width_two, dtype=jnp.float32)
    coupling_mats = couplings(angular, channel_table)
    slot_width, r_one = slot_geometry(element_width, tile_offset, slot_count, slot_count)
    slot_ids = jnp.arange(slot_count, dtype=jnp.int32)
    live_slots = slot_ids < tile_count
    last_slot = slot_ids == tile_count - 1
    inner_slots = slot_ids + 1 < tile_count
    live_mask = live_slots[None, None, :, None, None]
    first_chan = lax.axis_index("chan") * local_chan
    own_table = lax.dynamic_slice_in_dim(channel_table, first_chan, local_chan, 0)
    potential = diagonal_terms(own_table, r_one, r_two)
    weights = radial_weights(r_one, r_two)
    kinetic = element_kinetic[None] / (slot_width * slot_width)[:, None, None]
    own_rows = lax.dynamic_slice_in_dim(coupling_mats, first_chan, local_chan, 1)
    field = jnp.where(
        live_mask, wave.astype(jnp.float32).reshape(local_chan, 2, slot_count, PTS, width_two), 0.0
    )

    def local_terms(values, from_above, send_back):
        inner_next = jnp.concatenate(
            [values[:, :, 1:, 0, :], jnp.zeros_like(values[:, :, :1, 0, :])], axis=2
        )
        next_rows = jnp.where(
            inner_slots[None, None, :, None],
            inner_next,
            jnp.where(last_slot[None, None, :, None], from_above[:, :, None, :], 0.0),
        )
        block = jnp.concatenate([values, next_rows[:, :, :, None, :]], axis=3)
        element_out = jnp.einsum("gqp,cxgpr->cxgqr", kinetic, block, precision=highest)
        spill_terms = element_out[:, :, :, PTS, :]
        outgoing = jnp.sum(jnp.where(last_slot[None, None, :, None], spill_terms, 0.0), axis=2)
        from_below = send_back(outgoing)
        inner_spill = jnp.where(inner_slots[None, None, :, None], spill_terms, 0.0)
        spill_in = jnp.concatenate([from_below[:, :, None, :], inner_spill[:, :, :-1, :]], axis=2)
        result = element_out[:, :, :, :PTS, :].at[:, :, :, 0, :].add(spill_in)
        result = result + jnp.einsum("cxgpr,rs->cxgps", values, radial_two, precision=highest)
        return result + potential[:, None] * values

    def apply_ham(values):
        from_above = from_behind(values[:, :, 0, 0, :].astype(jnp.bfloat16), "rad", -1).astype(
            jnp.float32
        )

        def send_back(outgoing):
            return from_behind(as_sent(outgoing), "rad", 1).astype(outgoing.dtype)

        result = local_terms(values, from_above, send_back)
        running_sum = jnp.zeros_like(values)
        chan_piece = lax.all_gather(values.astype(jnp.bfloat16), "chan", axis=0, tiled=True).astype(
            jnp.float32
        )
        for multipole in range(LAM):
            coeff_block = own_rows[multipole]
            running_sum = running_sum + jnp.einsum(
                "cd,dxgpr->cxgpr", coeff_block, weights[multipole] * chan_piece, precision=highest
            )
        return jnp.where(live_mask, result + running_sum, 0.0)

    evolved = propagate(field, apply_ham)
    return evolved.reshape(wave.shape)


def solution(mesh):
    in_specs = (P("chan", None, "rad", "grp"), P(("grp", "rad")), P("grp"), P(), P(), P(), P())
    out_specs = P("chan", None, "rad", "grp")
    return jax.shard_map(
        per_device, mesh=mesh, in_specs=in_specs, out_specs=out_specs, check_vma=False
    )
```

profile of v0, /device:TPU:26, one launch (start us, length us, event | category | flops | bytes accessed | tf_op | source)
XLA Modules:
  0.0 91.3 jit_solution(9601986390322342957)
XLA Ops:
  6.5 0.0 copy-start
  6.5 0.0 all-gather.2.cloned.1.call-start
  7.3 2.2 %copy_convert_fusion = f32[32,2,30,512]{3,0,2,1:T(8,128)S(1)} fusion(bf16[32,2,30,512]{3,1,2,0:T(2,128)(2,1)} %param.11), kind=kLoop, calls=%fused_computation.14 | loop fusion | flops 983040 | bytes 5898240 | tf_op jit(solution)/shard_map/convert_element_type | solution.py:134
  9.5 0.0 copy-start.8
  9.5 0.0 copy-start.6
  9.5 0.0 copy-start.4
  9.5 0.0 copy-start.7
  9.5 3.5 %fusion.51 = (bf16[32,2,2,15,512]{4,0,3,2,1:T(8,128)(2,1)}, f32[32,2,2,15,512]{4,0,3,2,1:T(8,128)}) fusion(f32[32,2,2,15,512]{4,0,3,2,1:T(8,128)S(1)} %bitcast.110, pred[2]{0:T(512)(128)(4,1)S(1)} %iota_compare_fusion.1), kind=kLoop, calls=%fused_computation.120 | loop fusion | flops 1966080 | bytes 9830402 | tf_op jit(solution)/shard_map/convert.1
  13.0 0.0 all-gather.2.cloned.1.call-update
  13.0 0.8 slice_bitcast_fusion.3
  13.9 3.3 %collective-permute-start = (bf16[32,2,512]{2,0,1:T(8,128)(2,1)S(1)}, bf16[32,2,512]{2,0,1:T(8,128)(2,1)S(1)}, u32[]{:S(2)}, u32[]{:S(2)}) collective-permute-start(bf16[32,2,512]{2,0,1:T(8,128)(2,1)S(1)} %slice_bitcast_fusion.3), channel_id=1, source_target_pairs={{2,0},{4,2},{6,4},{8,6},{10,8},{12,10},{14,12},{3,1},{5,3},{7,5},{... | collective-permute-start | bytes 196616 | tf_op jit(solution)/shard_map/ppermute | solution.py:31
  17.3 0.0 copy-done.8
  17.3 0.6 dynamic-slice.8
  17.9 0.7 dynamic-update-slice.3
  18.6 7.6 %all-reduce.3 = s32[8]{0:T(128)S(1)} all-reduce(s32[8]{0:T(128)S(1)} %dynamic-update-slice.3), channel_id=1, replica_groups=mesh['grp'=2,'rad'=8,'chan'=2] {'rad'}, use_global_device_ids=true, to_apply=%add.3 | all-reduce | flops 8 | bytes 64
  26.3 7.0 %while.11 = (s32[]{:T(128)}, s32[]{:T(128)}, s32[]{:T(128)}, s32[8]{0:T(128)S(1)}, s32[]{:T(128)}, /*index=5*/s32[]{:T(128)}, s32[]{:T(128)}) while((s32[]{:T(128)}, s32[]{:T(128)}, s32[]{:T(128)}, s32[8]{0:T(128)S(1)}, s32[]{:T(128)}, /*index=5*/s32[]{:T(128)}, s32[]{:T(128)}) %tuple.32), condition=%wide.region_1.2_spmd, body=%wide.region_0.1_spmd.sunk | while | flops 6 | bytes 135 | solution.py:25
  26.3 0.6 dynamic_slice.33
  27.4 0.6 dynamic_slice.33
  28.6 0.6 dynamic_slice.33
  29.8 0.6 dynamic_slice.33
  31.0 0.6 dynamic_slice.33
  32.1 0.6 dynamic_slice.33
  33.3 0.0 copy-done.6
  33.3 0.1 constant_dynamic-slice_fusion
  33.4 0.0 copy-done.4
  33.4 0.1 copy.54
  33.5 0.1 copy.55
  33.5 0.0 copy-done.7
  33.6 0.1 fusion.50
  33.6 0.2 reduce-window.9
  33.8 0.1 pad_maximum_fusion.1
  33.9 0.2 fusion.28
  34.1 0.1 dynamic-slice_add_fusion
  34.2 0.1 broadcast_in_dim.104
  34.2 0.1 broadcast_in_dim.105
  34.3 0.1 fusion.49
  34.4 0.1 broadcast_multiply_fusion.1
  34.5 0.1 broadcast_multiply_fusion
  34.6 0.1 add_multiply_fusion
  34.6 0.1 fusion.10
  34.7 0.9 %slice_bitcast_fusion.2 = f32[32,2,1,512]{3,0,2,1:T(8,128)S(1)} fusion(f32[32,2,2,15,512]{4,0,3,2,1:T(8,128)} %get-tuple-element.55), kind=kLoop, calls=%fused_computation.26 | loop fusion | bytes 262144 | tf_op jit(solution)/shard_map/squeeze | solution.py:139
  35.7 0.2 add_subtract_fusion
  35.9 0.0 collective-permute-done
  36.0 0.1 select_bitcast_fusion
  36.1 0.0 copy-start.5
  36.1 2.6 %pad_maximum_fusion = f32[32,2,2,16,512]{4,0,3,2,1:T(8,128)S(1)} fusion(f32[32,2,2,1,512]{4,0,3,2,1:T(8,128)S(1)} %select_bitcast_fusion, f32[32,2,2,15,512]{4,0,3,2,1:T(8,128)} %get-tuple-element.55), kind=kLoop, calls=%fused_computation.4 | loop fusion | flops 1048576 | bytes 8388608 | tf_op jit(solution)/shard_map/concatenate | solution.py:146
  38.7 6.5 %fusion.2 = f32[2,32,2,512,16]{3,4,2,1,0:T(8,128)S(1)} fusion(f32[32,2,2,16,512]{4,0,3,2,1:T(8,128)S(1)} %pad_maximum_fusion, f32[2]{0:T(128)S(1)} %get-tuple-element.52, f32[16,16]{1,0:T(8,128)S(1)} %copy-done.5), kind=kOutput, calls=%fused_computation.6 | convolution fusion | flops 201327104 | bytes 8389640 | tf_op jit(solution)/shard_map/gqp,cxgpr->cxgqr/dot_general | solution.py:147
  45.2 2.4 %copy.64 = f32[2,32,2,512,16]{3,1,0,2,4:T(8,128)S(1)} copy(f32[2,32,2,512,16]{3,4,2,1,0:T(8,128)S(1)} %fusion.2) | data formatting | bytes 8388608 | tf_op jit(solution)/shard_map/gqp,cxgpr->cxgqr/dot_general | solution.py:147
  47.7 0.1 select_reduce_fusion
  47.7 4.5 %collective-permute-start.1 = (bf16[32,2,512]{2,0,1:T(8,128)(2,1)S(1)}, bf16[32,2,512]{2,0,1:T(8,128)(2,1)S(1)}, u32[]{:S(2)}, u32[]{:S(2)}) collective-permute-start(bf16[32,2,512]{2,0,1:T(8,128)(2,1)S(1)} %select_reduce_fusion), channel_id=1, source_target_pairs={{0,2},{2,4},{4,6},{6,8},{8,10},{10,12},{12,14},{1,3},{3,5},{5,7},{... | collective-permute-start | bytes 196616 | tf_op jit(solution)/shard_map/ppermute | solution.py:31
  52.3 0.7 slice.103
  53.0 2.3 %copy.43 = f32[32,2,2,15,512]{4,0,3,2,1:T(8,128)} copy(f32[32,2,2,15,512]{4,0,2,1,3:T(8,128)S(1)} %slice.103) | data formatting | bytes 7864320 | tf_op jit(solution)/shard_map/slice | solution.py:153
  55.4 0.0 collective-permute-done.1
  55.4 0.7 fusion.9
  56.1 6.7 %fusion.1 = f32[32,2,2,15,512]{4,0,3,2,1:T(8,128)S(1)} fusion(bf16[64,2,2,15,512]{4,0,3,2,1:T(8,128)(2,1)} %all-gather.2.cloned.1.call-done, f32[2,15,512]{2,1,0:T(8,128)S(1)} %get-tuple-element.62, f32[2,32,64]{2,1,0:T(8,128)S(1)} %fusion.23), kind=kOutput, calls=%fused_computation.3 | convolution fusion | flops 758906880 | bytes 7946240 | tf_op jit(solution)/shard_map/cd,dxgpr->cxgpr/dot_general | solution.py:172
  62.8 0.0 copy-done.2
  62.9 0.0 copy-start.1
  62.9 4.5 %fusion = f32[32,2,2,15,512]{4,0,3,2,1:T(8,128)S(1)} fusion(bf16[64,2,2,15,512]{4,0,3,2,1:T(8,128)(2,1)S(1)} %copy-done.2, f32[2,15,512]{2,1,0:T(8,128)S(1)} %get-tuple-element.63, f32[2,32,64]{2,1,0:T(8,128)S(1)} %fusion.23), kind=kOutput, calls=%fused_computation.2 | convolution fusion | flops 758906880 | bytes 7946240 | tf_op jit(solution)/shard_map/cd,dxgpr->cxgpr/dot_general | solution.py:172
  67.4 9.5 %add_select_fusion = f32[32,2,2,15,512]{4,0,3,2,1:T(8,128)S(1)} fusion(f32[32,2,2,15,512]{4,0,3,2,1:T(8,128)S(1)} %fusion, f32[32,2,2,15,512]{4,0,3,2,1:T(8,128)S(1)} %fusion.1, f32[32,2,2,15,512]{4,0,3,2,1:T(8,128)S(1)} %copy-done.1, f32[32,2,2,15,512]{4,0,3,2,1:T(8,128)} %fusion.9, f32[32,2,15,512]{3,0,2,1:T(8,128)S(1)} %add_subtract_fusion, ...), kind=kOutput, calls=%fused_computation.10 | convolution fusion | flops 6045696000 | bytes 22675458 | tf_op jit(solution)/shard_map/cxgpr,rs->cxgps/dot_general | solution.py:154
  76.9 0.0 copy-start.3
  76.9 0.8 fusion.52
  77.7 0.7 copy-done.3
  78.4 1.1 %fusion.4 = f32[32,2,30,512]{3,0,2,1:T(8,128)S(1)} fusion(f32[32,1,30,512]{3,0,2,1:T(8,128)S(1)} %bitcast.112, f32[32,1,30,512]{3,0,2,1:T(8,128)S(1)} %bitcast.111, pred[30]{0:T(512)(128)(4,1)S(1)} %broadcast_in_dim.105, bf16[32,2,30,512]{3,1,2,0:T(2,128)(2,1)S(1)} %copy-done.3), kind=kLoop, calls=%fused_computation.9 | loop fusion | flops 4915200 | bytes 9830430 | tf_op jit(solution)/shard_map/add | solution.py:90
  79.5 5.0 %copy.48 = f32[32,2,30,512]{3,1,2,0:T(2,128)} copy(f32[32,2,30,512]{3,0,2,1:T(8,128)S(1)} %fusion.4) | data formatting | bytes 7864320 | tf_op jit(solution)/shard_map/add | solution.py:90
  (21 shorter events, 0.2 us)
Async XLA Ops:
  6.5 60.8 %copy-start = (f32[512,512]{1,0:T(8,128)S(1)}, f32[512,512]{1,0:T(8,128)}, u32[]{:S(2)}) copy-start(f32[512,512]{1,0:T(8,128)} %param.15) | copy-start | bytes 3145732
  6.5 49.6 %all-gather.2.cloned.1.call-start = ((), (), s32[]{:S(2)}) async-start(), calls=%async_computation | async-start | bytes 5898240 | tf_op jit(solution)/shard_map/all_gather | solution.py:167
  9.5 7.8 %copy-start.8 = (u32[32]{0:T(128)S(1)}, u32[32]{0:T(128)}, u32[]{:S(2)}) copy-start(u32[32]{0:T(128)} %constant.128) | copy-start | bytes 388
  9.5 23.8 %copy-start.6 = (s32[64,2]{0,1:T(2,128)S(1)}, s32[64,2]{0,1:T(2,128)}, u32[]{:S(2)}) copy-start(s32[64,2]{0,1:T(2,128)} %param.17) | copy-start | bytes 1540
  9.5 23.9 %copy-start.4 = (f32[2,64,64]{2,1,0:T(8,128)S(1)}, f32[2,64,64]{2,1,0:T(8,128)}, u32[]{:S(2)}) copy-start(f32[2,64,64]{2,1,0:T(8,128)} %param.16) | copy-start | bytes 98308
  9.5 24.1 %copy-start.7 = (f32[12]{0:T(128)S(1)}, f32[12]{0:T(128)}, u32[]{:S(2)}) copy-start(f32[12]{0:T(128)} %param.13) | copy-start | bytes 148
  13.9 22.1 %collective-permute-start = (bf16[32,2,512]{2,0,1:T(8,128)(2,1)S(1)}, bf16[32,2,512]{2,0,1:T(8,128)(2,1)S(1)}, u32[]{:S(2)}, u32[]{:S(2)}) collective-permute-start(bf16[32,2,512]{2,0,1:T(8,128)(2,1)S(1)} %slice_bitcast_fusion.3), channel_id=1, source_target_pairs={{2,0},{4,2},{6,4},{8,6},{10,8},{12,10},{14,12},{3,1},{5,3},{7,5},{... | collective-permute-start | bytes 196616 | tf_op jit(solution)/shard_map/ppermute | solution.py:31
  36.1 2.6 %copy-start.5 = (f32[16,16]{1,0:T(8,128)S(1)}, f32[16,16]{1,0:T(8,128)}, u32[]{:S(2)}) copy-start(f32[16,16]{1,0:T(8,128)} %param.14) | copy-start | bytes 3076
  47.7 7.6 %collective-permute-start.1 = (bf16[32,2,512]{2,0,1:T(8,128)(2,1)S(1)}, bf16[32,2,512]{2,0,1:T(8,128)(2,1)S(1)}, u32[]{:S(2)}, u32[]{:S(2)}) collective-permute-start(bf16[32,2,512]{2,0,1:T(8,128)(2,1)S(1)} %select_reduce_fusion), channel_id=1, source_target_pairs={{0,2},{2,4},{4,6},{6,8},{8,10},{10,12},{12,14},{1,3},{3,5},{5,7},{... | collective-permute-start | bytes 196616 | tf_op jit(solution)/shard_map/ppermute | solution.py:31
  56.1 6.7 %copy-start.2 = (bf16[64,2,2,15,512]{4,0,3,2,1:T(8,128)(2,1)S(1)}, bf16[64,2,2,15,512]{4,0,3,2,1:T(8,128)(2,1)}, u32[]{:S(2)}) copy-start(bf16[64,2,2,15,512]{4,0,3,2,1:T(8,128)(2,1)} %all-gather.2.cloned.1.call-done) | copy-start | bytes 11796484
  62.9 4.5 %copy-start.1 = (f32[32,2,2,15,512]{4,0,3,2,1:T(8,128)S(1)}, f32[32,2,2,15,512]{4,0,3,2,1:T(8,128)}, u32[]{:S(2)}) copy-start(f32[32,2,2,15,512]{4,0,3,2,1:T(8,128)} %get-tuple-element.55) | copy-start | bytes 11796484
  76.9 1.5 %copy-start.3 = (bf16[32,2,30,512]{3,1,2,0:T(2,128)(2,1)S(1)}, bf16[32,2,30,512]{3,1,2,0:T(2,128)(2,1)}, u32[]{:S(2)}) copy-start(bf16[32,2,30,512]{3,1,2,0:T(2,128)(2,1)} %param.11) | copy-start | bytes 5898244
Sparse Core Ops, SparseCore 0:
  13.1 14.4 all-gather.1
where the time goes:
time: 91.7 us; the launch traced here: 91.3 us
  matrix products  27.2 us (30%)
  local copies, waits for them, and re-layouts  18.2 us (20%)
  between operations  14.5 us (16%)
  other arithmetic  12.4 us (14%)
  starting transfers between devices  7.78 us (8%)
  blocking collectives  7.64 us (8%)
  loops' own time  3.51 us (4%)
    dot_general x2, matrix products, apply_ham(): jnp.einsum('cd,dxgpr->cxgpr', coeff_block, weights[multipole] * chan_piec...  11.2 us
    dot_general x1, matrix products, local_terms(): jnp.einsum('cxgpr,rs->cxgps', values, radial_two, precision=highest)  9.49 us
    ppermute x2, starting transfers between devices, from_behind(): lax.ppermute(value, axis, [(source, source + steps) for source in range(l...  7.77 us
    unnamed x1, blocking collectives  7.64 us
    dot_general x1, matrix products, local_terms(): jnp.einsum('gqp,cxgpr->cxgqr', kinetic, block, precision=highest)  6.53 us
    add x1, local copies, waits for them, and re-layouts, propagate(): running = running + taylor_term  4.96 us
    another operation x2, other arithmetic  3.67 us
    another operation x1, loops' own time, carried_in(): return lax.fori_loop(0, place, one, state)  3.51 us
  transfers between devices with their start and end apart: 3, of which 0 were waited for; matrix products, arithmetic and copies ran while one was open for 26% of the time, Pallas kernels for 0%

commit v1 on v0

v1 whole, which is shorter than its diff:
```python
import functools

import jax
import jax.numpy as jnp
from jax import lax
from jax.experimental import pallas as pl
from jax.experimental.pallas import tpu as pltpu
from jax.sharding import PartitionSpec as P

PTS = 15
SLOTS = 2
MESH = pl.DeviceIdType.MESH
highest = lax.Precision.HIGHEST
charge = 2.0
inner_radius = 4.0
radial_step = 0.1
time_step = 0.1


def mm(a, b):
    return jnp.dot(a, b, preferred_element_type=jnp.float32)


def two_parts(a):
    high = a.astype(jnp.bfloat16)
    return high, (a - high.astype(jnp.float32)).astype(jnp.bfloat16)


def kron_parts(small, outer, inner, small_outer):
    size = outer * inner
    width = small.shape[0]
    row = lax.broadcasted_iota(jnp.int32, (size, width), 0)
    col = lax.broadcasted_iota(jnp.int32, (size, width), 1)
    pick_r = ((row // inner if small_outer else row % inner) == col).astype(jnp.float32)
    row = lax.broadcasted_iota(jnp.int32, (width, size), 0)
    col = lax.broadcasted_iota(jnp.int32, (width, size), 1)
    pick_c = ((col // inner if small_outer else col % inner) == row).astype(jnp.float32)
    spread = jnp.dot(pick_r, small, precision=highest, preferred_element_type=jnp.float32)
    spread = jnp.dot(spread, pick_c, precision=highest, preferred_element_type=jnp.float32)
    row = lax.broadcasted_iota(jnp.int32, (size, size), 0)
    col = lax.broadcasted_iota(jnp.int32, (size, size), 1)
    keep = (row % inner == col % inner) if small_outer else (row // inner == col // inner)
    return two_parts(jnp.where(keep, spread, 0.0))


def kernel(
    n_rad, v, count, widths, fractions, kin_s, kin_v, rtwo, m_own, m_oth, coef, out,
    other, next_in, below, spill, counts, kin, acc,
    c_send, c_recv, k_send, k_recv, e_send, e_recv,
):
    channels, width_two = v.shape[2], v.shape[3]
    me_rad = lax.axis_index("rad")
    me_chan = lax.axis_index("chan")
    partner = 1 - me_chan
    rad_of = [lax.rem(me_rad + k, n_rad) for k in range(n_rad)]

    barrier = pltpu.get_barrier_semaphore()
    pl.semaphore_signal(barrier, inc=1, device_id={"chan": partner}, device_id_type=MESH)
    for k in range(1, n_rad):
        pl.semaphore_signal(barrier, inc=1, device_id={"rad": rad_of[k]}, device_id_type=MESH)
    pl.semaphore_wait(barrier, n_rad)

    count_copies = []
    for k in range(1, n_rad):
        copy = pltpu.make_async_remote_copy(
            src_ref=count, dst_ref=counts.at[k], send_sem=k_send.at[k], recv_sem=k_recv.at[k],
            device_id={"rad": rad_of[k]}, device_id_type=MESH)
        copy.start()
        count_copies.append(copy)
    field_copies = {}
    for g in range(SLOTS):
        for x in range(2):
            part = (x, pl.ds(g * PTS, PTS))
            copy = pltpu.make_async_remote_copy(
                src_ref=v.at[part], dst_ref=other.at[part], send_sem=c_send.at[x, g],
                recv_sem=c_recv.at[x, g], device_id={"chan": partner}, device_id_type=MESH)
            copy.start()
            field_copies[x, g] = copy
    edge_copies = []
    for x in range(2):
        copy = pltpu.make_async_remote_copy(
            src_ref=v.at[x, 0], dst_ref=next_in.at[x], send_sem=e_send.at[x], recv_sem=e_recv.at[x],
            device_id={"rad": rad_of[n_rad - 1]}, device_id_type=MESH)
        copy.start()
        edge_copies.append(copy)

    k_high, k_low = kron_parts(kin_v[...], 16, 16, True)
    k_high, k_low = k_high[:, :PTS * 16], k_low[:, :PTS * 16]
    for g in range(SLOTS):
        for x in range(2):
            for cb in range(channels // 16):
                block = v[x, g * PTS:(g + 1) * PTS, cb * 16:(cb + 1) * 16, :].reshape(PTS * 16, width_two)
                res = mm(k_high, block) + mm(k_low, block)
                kin[x, g, :, cb * 16:(cb + 1) * 16, :] = res.reshape(16, 16, width_two)

    own_count = count[0:1, 0:1]
    two_slots = own_count >= 2
    for x in range(2):
        spill[x] = jnp.where(two_slots, kin[x, 1, PTS], kin[x, 0, PTS]).astype(jnp.bfloat16)
        copy = pltpu.make_async_remote_copy(
            src_ref=spill.at[x], dst_ref=below.at[x], send_sem=e_send.at[2 + x], recv_sem=e_recv.at[2 + x],
            device_id={"rad": rad_of[1]}, device_id_type=MESH)
        copy.start()
        edge_copies.append(copy)

    blocks = [(0, 8), (8, 7)]
    r_high, r_low = two_parts(rtwo[...])
    for g in range(SLOTS):
        for x in range(2):
            for p0, size in blocks:
                rows = pl.ds(g * PTS + p0, size)
                block = v[x, rows].reshape(size * channels, width_two)
                acc[x, rows] = (mm(block, r_high) + mm(block, r_low)).reshape(size, channels, width_two)
    own_high, own_low = kron_parts(m_own[...], 8, channels, False)
    oth_high, oth_low = kron_parts(m_oth[...], 8, channels, False)

    for copy in count_copies:
        copy.wait()
    offset = jnp.zeros((1, 1), jnp.int32)
    for k in range(1, n_rad):
        offset = offset + jnp.where(k <= me_rad, counts[k, 0:1, 0:1], 0)
    element = lax.broadcasted_iota(jnp.int32, widths.shape, 1)
    all_widths = widths[...]

    def width_at(index):
        found = jnp.sum(jnp.where(element == index, all_widths, 0.0), axis=1, keepdims=True)
        return jnp.where(found > 0.0, found, 1.0)

    r_two = inner_radius + radial_step * lax.broadcasted_iota(jnp.int32, (1, width_two), 1).astype(jnp.float32)
    inv_two = 1.0 / r_two
    first_l, second_l, mono = coef[:, 0:1], coef[:, 1:2], coef[:, 2:3]
    base = second_l * (inv_two * inv_two) - charge * inv_two

    for copy in edge_copies:
        copy.wait()
    inv_below = 1.0 / width_at(offset - 1)
    inv_below = jnp.where(me_rad > 0, inv_below * inv_below, 0.0)
    corner = kin_s[PTS, PTS]
    above = [jnp.where(me_rad < n_rad - 1, next_in[x].astype(jnp.float32), 0.0) for x in range(2)]
    inv_first = 1.0 / width_at(offset)
    inv_first = inv_first * inv_first
    for g in range(SLOTS):
        slot_width = width_at(offset + g)
        inv_w2 = 1.0 / slot_width
        inv_w2 = inv_w2 * inv_w2
        start = jnp.sum(jnp.where(element < offset + g, all_widths, 0.0), axis=1, keepdims=True)
        r_one = inner_radius + start + slot_width * fractions[:, 0:1]
        inv_one = 1.0 / r_one
        inv_far = 1.0 / jnp.maximum(r_one, r_two)
        weight = jnp.minimum(r_one, r_two) * inv_far * inv_far
        live = own_count > g
        for x in range(2):
            field_copies[x, g].wait()
            if g == 0:
                after = jnp.where(two_slots, v[x, PTS].astype(jnp.float32), above[x])
            else:
                after = above[x]
            after = after * inv_w2
            for p0, size in blocks:
                rows = pl.ds(g * PTS + p0, size)
                count_rows = size * channels
                mine = v[x, rows].reshape(count_rows, width_two)
                theirs = other[x, rows].reshape(count_rows, width_two)
                mix = mm(own_high[:count_rows, :count_rows], mine)
                mix = mix + mm(own_low[:count_rows, :count_rows], mine)
                mix = mix + mm(oth_high[:count_rows, :count_rows], theirs)
                mix = mix + mm(oth_low[:count_rows, :count_rows], theirs)
                for i in range(size):
                    q = p0 + i
                    row = g * PTS + q
                    mine_q = v[x, row].astype(jnp.float32)
                    potential = base + mono * inv_far[q:q + 1, :] + (
                        first_l * (inv_one[q:q + 1] * inv_one[q:q + 1]) - charge * inv_one[q:q + 1])
                    total = acc[x, row] + kin[x, g, q] * inv_w2 + kin_s[q, PTS] * after
                    total = total + potential * mine_q
                    total = total + weight[q:q + 1, :] * mix[i * channels:(i + 1) * channels]
                    if q == 0:
                        if g == 0:
                            total = total + (below[x].astype(jnp.float32) + corner * mine_q) * inv_below
                        else:
                            total = total + (kin[x, 0, PTS] + corner * mine_q) * inv_first
                    step = time_step if x == 1 else -time_step
                    result = v[1 - x, row].astype(jnp.float32) + step * total
                    out[1 - x, row] = jnp.where(live, result, 0.0)


def per_device(n_rad, wave, tile_elems, element_width, element_kinetic, radial_two, angular, channel_table):
    channels, _, rows, width_two = wave.shape
    field = wave.transpose(1, 2, 0, 3)
    count = jnp.broadcast_to(tile_elems[:, None], (8, 128))
    total = element_width.shape[0]
    lanes = -(-total // 128) * 128
    widths = jnp.pad(element_width, (0, lanes - total))[None, :]
    fractions = 0.5 * (1.0 - jnp.cos(jnp.pi * jnp.arange(16, dtype=jnp.float32) / PTS))
    fractions = jnp.broadcast_to(fractions[:, None], (16, 128))
    me = lax.axis_index("chan")
    own = lax.dynamic_slice_in_dim(channel_table, me * channels, channels, 0)
    oth = lax.dynamic_slice_in_dim(channel_table, (1 - me) * channels, channels, 0)

    def allowed(a, b):
        low = jnp.abs(a[:, None] - b[None, :])
        high = a[:, None] + b[None, :]
        return (low <= 1) & (1 <= high) & ((high + 1) % 2 == 0)

    def coupling(cols, first):
        keep = allowed(own[:, 0], cols[:, 0]) & allowed(own[:, 1], cols[:, 1])
        there = lax.dynamic_slice(angular[1], (me * channels, first), (channels, channels))
        back = lax.dynamic_slice(angular[1], (first, me * channels), (channels, channels))
        return jnp.where(keep, 0.5 * (there + back.T), 0.0)

    m_own = coupling(own, me * channels)
    m_oth = coupling(oth, (1 - me) * channels)
    block = lax.dynamic_slice(angular[0], (me * channels, me * channels), (channels, channels))
    mono = jnp.sum(jnp.where(jnp.eye(channels, dtype=bool), block, 0.0), axis=1)
    orbital = own.astype(jnp.float32)
    centri = 0.5 * orbital * (orbital + 1.0)
    coef = jnp.concatenate([centri, mono[:, None]], axis=1)

    vmem = pl.BlockSpec(memory_space=pltpu.VMEM)
    smem = pl.BlockSpec(memory_space=pltpu.SMEM)
    moved = pl.pallas_call(
        functools.partial(kernel, n_rad),
        out_shape=jax.ShapeDtypeStruct((2, rows, channels, width_two), jnp.float32),
        in_specs=[vmem, vmem, vmem, vmem, smem, vmem, vmem, vmem, vmem, vmem],
        out_specs=vmem,
        scratch_shapes=[
            pltpu.VMEM((2, rows, channels, width_two), jnp.bfloat16),
            pltpu.VMEM((2, channels, width_two), jnp.bfloat16),
            pltpu.VMEM((2, channels, width_two), jnp.bfloat16),
            pltpu.VMEM((2, channels, width_two), jnp.bfloat16),
            pltpu.VMEM((n_rad, 8, 128), jnp.int32),
            pltpu.VMEM((2, SLOTS, 16, channels, width_two), jnp.float32),
            pltpu.VMEM((2, rows, channels, width_two), jnp.float32),
            pltpu.SemaphoreType.DMA((2, SLOTS)),
            pltpu.SemaphoreType.DMA((2, SLOTS)),
            pltpu.SemaphoreType.DMA((n_rad,)),
            pltpu.SemaphoreType.DMA((n_rad,)),
            pltpu.SemaphoreType.DMA((4,)),
            pltpu.SemaphoreType.DMA((4,)),
        ],
        compiler_params=pltpu.CompilerParams(
            collective_id=0, has_side_effects=True, vmem_limit_bytes=44 * 1024 * 1024),
        cost_estimate=pl.CostEstimate(flops=6_000_000_000, bytes_accessed=10_000_000, transcendentals=0),
    )(field, count, widths, fractions, element_kinetic, element_kinetic, radial_two, m_own, m_oth, coef)
    return moved.transpose(2, 0, 1, 3)


def solution(mesh):
    in_specs = (P("chan", None, "rad", "grp"), P(("grp", "rad")), P("grp"), P(), P(), P(), P())
    out_specs = P("chan", None, "rad", "grp")
    return jax.shard_map(
        functools.partial(per_device, mesh.shape["rad"]), mesh=mesh, in_specs=in_specs,
        out_specs=out_specs, check_vma=False)
```

time: 91.7 us -> 28.1 us (0.31)
  the two profiles are of different devices: /device:TPU:26 before, /device:TPU:0 now
where the time goes in v1:
time: 28.1 us; the launch traced here: 27.9 us
  Pallas kernels  16.5 us (59%)
  local copies, waits for them, and re-layouts  9.55 us (34%)
  other arithmetic  1.02 us (4%)
  between operations  0.79 us (3%)
    pallas_call x1, Pallas kernels, per_device(): pl.pallas_call(functools.partial(kernel, n_rad), out_shape=jax.ShapeDtype...  16.5 us
    transpose x1, local copies, waits for them, and re-layouts, per_device(): return moved.transpose(2, 0, 1, 3)  4.96 us
    unnamed x5, local copies, waits for them, and re-layouts  2.01 us
    slice x1, local copies, waits for them, and re-layouts, per_device(): angular[0]  0.78 us
    dynamic_slice x1, local copies, waits for them, and re-layouts, per_device(): lax.dynamic_slice_in_dim(channel_table, (1 - me) * channels, channels, 0)  0.76 us
    mul x1, other arithmetic, per_device(): centri = 0.5 * orbital * (orbital + 1.0)  0.75 us
    broadcast_in_dim x1, local copies, waits for them, and re-layouts, per_device(): widths = jnp.pad(element_width, (0, lanes - total))[None, :]  0.66 us

profile of v1, /device:TPU:0, one launch (start us, length us, event | category | flops | bytes accessed | tf_op | source)
XLA Modules:
  0.0 27.9 jit_solution(17713504620351491342)
XLA Ops:
  0.0 0.0 copy-start
  0.0 0.0 copy-start.1
  0.7 0.7 %pad_bitcast_fusion.widths = f32[1,128]{1,0:T(1,128)S(1)} fusion(f32[12]{0:T(128)} %param.9), kind=kLoop, calls=%fused_computation.67 | loop fusion | bytes 560 | tf_op jit(solution)/shard_map/broadcast_in_dim | solution.py:193
  1.5 0.8 %constant_dynamic-slice_fusion.1 = s32[32,2]{0,1:T(2,128)S(1)} fusion(s32[64,2]{0,1:T(2,128)} %param.13, s32[]{:T(128)S(6)} %select_n.49), kind=kLoop, calls=%fused_computation.58 | loop fusion | bytes 516 | tf_op jit(solution)/shard_map/dynamic_slice | solution.py:198
  2.2 0.8 %add_multiply_fusion = (f32[32,2]{0,1:T(2,128)S(1)}, s32[32,2]{0,1:T(2,128)S(1)}) fusion(s32[64,2]{0,1:T(2,128)} %param.13, s32[]{:T(128)S(6)} %select_n.45), kind=kLoop, calls=%fused_computation.61 | loop fusion | flops 256 | bytes 772 | tf_op jit(solution)/shard_map/mul | solution.py:216
  3.0 0.1 broadcast_in_dim.29.fractions
  3.0 0.8 %fusion.27 = (f32[1,64,64]{2,1,0:T(8,128)S(1)}, f32[1,64,64]{2,1,0:T(8,128)S(1)}) fusion(f32[2,64,64]{2,1,0:T(8,128)} %param.12), kind=kLoop, calls=%fused_computation.68 | loop fusion | bytes 65536 | tf_op jit(solution)/shard_map/slice | solution.py:213
  3.8 0.1 constant_dynamic-slice_fusion
  3.9 0.1 copy.25
  4.0 0.1 copy.23
  4.0 0.2 fusion.13
  4.3 0.1 copy.26.coef
  4.4 2.0 %copy.30 = bf16[32,2,30,512]{3,0,2,1:T(8,128)(2,1)S(1)} copy(bf16[32,2,30,512]{3,1,2,0:T(2,128)(2,1)} %param.7) | data formatting | bytes 3932160 | tf_op args[0]
  6.4 0.0 copy-done
  6.4 0.0 copy-done.1
  6.4 16.5 %shard_map.73 = f32[2,30,32,512]{3,2,1,0:T(8,128)S(1)} custom-call(bf16[2,30,32,512]{3,2,1,0:T(8,128)(2,1)S(1)} %bitcast.42, s32[8,128]{1,0:T(8,128)S(1)} %broadcast_in_dim.27.count, f32[1,128]{1,0:T(1,128)S(1)} %pad_bitcast_fusion.widths, f32[16,128]{1,0:T(8,128)S(1)} %broadcast_in_dim.29.fractions, f32[16,16]{1,0:T(8,128)S(1)} %copy-done.1, ...), custom_call_target="tpu_custom_call" | custom-call | flops 6000000000 | bytes 10000000 | tf_op jit(solution)/shard_map/pallas_call | solution.py:221
  22.9 5.0 %copy.27 = f32[32,2,30,512]{3,1,2,0:T(2,128)} copy(f32[32,2,30,512]{3,0,2,1:T(8,128)S(1)} %bitcast.41) | data formatting | bytes 7864320 | tf_op jit(solution)/shard_map/transpose | solution.py:245
  (5 shorter events, 0.1 us)
Async XLA Ops:
  0.0 6.4 %copy-start = (f32[512,512]{1,0:T(8,128)S(1)}, f32[512,512]{1,0:T(8,128)}, u32[]{:S(2)}) copy-start(f32[512,512]{1,0:T(8,128)} %rtwo.1) | copy-start | bytes 3145732
  0.0 6.4 %copy-start.1 = (f32[16,16]{1,0:T(8,128)S(1)}, f32[16,16]{1,0:T(8,128)}, u32[]{:S(2)}) copy-start(f32[16,16]{1,0:T(8,128)} %kin_v.1) | copy-start | bytes 3076

commit v2 on v1

v2 whole, which is shorter than its diff:
```python
import functools
import math

import jax
import jax.numpy as jnp
from jax import lax
from jax.experimental import pallas as pl
from jax.experimental.pallas import tpu as pltpu
from jax.sharding import PartitionSpec as P

PTS = 15
SLOTS = 2
MESH = pl.DeviceIdType.MESH
highest = lax.Precision.HIGHEST
charge = 2.0
inner_radius = 4.0
radial_step = 0.1
time_step = 0.1


def mm(a, b):
    return jnp.dot(a, b, preferred_element_type=jnp.float32)


def two_parts(a):
    high = a.astype(jnp.bfloat16)
    return high, (a - high.astype(jnp.float32)).astype(jnp.bfloat16)


def one_hot(shape, index):
    return (index == lax.broadcasted_iota(jnp.int32, shape, 1)).astype(jnp.float32)


def rows_of(shape):
    return lax.broadcasted_iota(jnp.int32, shape, 0)


def cols_of(shape):
    return lax.broadcasted_iota(jnp.int32, shape, 1)


def spread(pick_rows, matrix, pick_cols):
    first = jnp.dot(pick_rows, matrix, precision=highest, preferred_element_type=jnp.float32)
    return lax.dot_general(
        first, pick_cols, (((1,), (1,)), ((), ())), precision=highest, preferred_element_type=jnp.float32)


def kinetic_parts(kinetic):
    pick = one_hot((256, 16), rows_of((256, 16)) // 16)
    keep = rows_of((256, 256)) % 16 == cols_of((256, 256)) % 16
    return two_parts(jnp.where(keep, spread(pick, kinetic, pick), 0.0))


def channel_parts(table, angular, me, channels, points):
    every = 2 * channels
    square = (every, every)
    eye = rows_of(square) == cols_of(square)
    keep = None
    for electron in range(2):
        row = table[electron:electron + 1, :].astype(jnp.float32)
        column = jnp.sum(jnp.where(eye, row, 0.0), axis=1, keepdims=True)
        apart = jnp.abs(column - row) == 1.0
        keep = apart if keep is None else keep & apart
    turned = lax.dot_general(
        eye.astype(jnp.float32), angular[1], (((1,), (1,)), ((), ())), precision=highest,
        preferred_element_type=jnp.float32)
    matrix = jnp.where(keep, 0.5 * (angular[1] + turned), 0.0)
    out_rows, in_rows = points * channels, points * every
    pick_r = one_hot((out_rows, every), me * channels + rows_of((out_rows, every)) % channels)
    pick_c = one_hot((in_rows, every), (rows_of((in_rows, every)) + me * channels) % every)
    same = rows_of((out_rows, in_rows)) // channels == cols_of((out_rows, in_rows)) // every
    return two_parts(jnp.where(same, spread(pick_r, matrix, pick_c), 0.0))


def own_columns(table, angular, me, channels):
    shape = (channels, 2 * channels)
    mine = rows_of(shape) + me * channels == cols_of(shape)

    def column(row):
        return jnp.sum(jnp.where(mine, row, 0.0), axis=1, keepdims=True)

    first = column(table[0:1, :].astype(jnp.float32))
    second = column(table[1:2, :].astype(jnp.float32))
    square = (2 * channels, 2 * channels)
    diagonal = jnp.where(rows_of(square) == cols_of(square), angular[0], 0.0)
    mono = column(jnp.sum(diagonal, axis=0, keepdims=True))
    return 0.5 * first * (first + 1.0), 0.5 * second * (second + 1.0), mono


def kernel(
    n_rad, raw, tile_elems, widths, kin_s, kin_v, rtwo, angular, table, out,
    full, next_in, below, spill, count, counts, kin, acc,
    c_send, c_recv, k_send, k_recv, e_send, e_recv,
):
    local_rows, channels, width_two = acc.shape[1:]
    lane_tiles = width_two // 128
    pitch = local_rows * lane_tiles * 2
    me_rad = lax.axis_index("rad")
    me_chan = lax.axis_index("chan")
    partner = 1 - me_chan
    rad_of = [lax.rem(me_rad + k, n_rad) for k in range(n_rad)]

    def place(x, row, tile):
        return pl.ds((row * lane_tiles + tile) * 2 + x, channels, stride=pitch)

    barrier = pltpu.get_barrier_semaphore()
    pl.semaphore_signal(barrier, inc=1, device_id={"chan": partner}, device_id_type=MESH)
    for k in range(1, n_rad):
        pl.semaphore_signal(barrier, inc=1, device_id={"rad": rad_of[k]}, device_id_type=MESH)
    count[...] = jnp.full(count.shape, tile_elems[0], jnp.int32)

    for c in range(0, channels, 4):
        out[c * pitch:(c + 4) * pitch, :] = raw[c * pitch:(c + 4) * pitch, :].astype(jnp.float32)

    def unpack(g):
        for row in range(g * PTS, (g + 1) * PTS):
            for x in range(2):
                for tile in range(lane_tiles):
                    full[x, row, 0:channels, tile * 128:(tile + 1) * 128] = out[
                        place(x, row, tile), :].astype(jnp.bfloat16)

    unpack(0)
    pl.semaphore_wait(barrier, n_rad)
    count_copies = []
    for k in range(1, n_rad):
        copy = pltpu.make_async_remote_copy(
            src_ref=count, dst_ref=counts.at[k], send_sem=k_send.at[k], recv_sem=k_recv.at[k],
            device_id={"rad": rad_of[k]}, device_id_type=MESH)
        copy.start()
        count_copies.append(copy)
    edge_copies = []
    for x in range(2):
        copy = pltpu.make_async_remote_copy(
            src_ref=full.at[x, 0, pl.ds(0, channels)], dst_ref=next_in.at[x], send_sem=e_send.at[x],
            recv_sem=e_recv.at[x], device_id={"rad": rad_of[n_rad - 1]}, device_id_type=MESH)
        copy.start()
        edge_copies.append(copy)
    field_copies = {}
    for g in range(SLOTS):
        if g > 0:
            unpack(g)
        for x in range(2):
            copy = pltpu.make_async_remote_copy(
                src_ref=full.at[x, pl.ds(g * PTS, PTS), pl.ds(0, channels)],
                dst_ref=full.at[x, pl.ds(g * PTS, PTS), pl.ds(channels, channels)],
                send_sem=c_send.at[x, g], recv_sem=c_recv.at[x, g],
                device_id={"chan": partner}, device_id_type=MESH)
            copy.start()
            field_copies[x, g] = copy

    k_high, k_low = kinetic_parts(kin_v[...])
    k_high, k_low = k_high[:, :PTS * 16], k_low[:, :PTS * 16]
    for g in range(SLOTS):
        for x in range(2):
            for cb in range(channels // 16):
                block = full[x, g * PTS:(g + 1) * PTS, cb * 16:(cb + 1) * 16, :].reshape(PTS * 16, width_two)
                res = mm(k_high, block) + mm(k_low, block)
                kin[x, g, :, cb * 16:(cb + 1) * 16, :] = res.reshape(16, 16, width_two)

    own_count = count[0:1, 0:1]
    two_slots = own_count >= 2
    for x in range(2):
        spill[x] = jnp.where(two_slots, kin[x, 1, PTS], kin[x, 0, PTS]).astype(jnp.bfloat16)
        copy = pltpu.make_async_remote_copy(
            src_ref=spill.at[x], dst_ref=below.at[x], send_sem=e_send.at[2 + x], recv_sem=e_recv.at[2 + x],
            device_id={"rad": rad_of[1]}, device_id_type=MESH)
        copy.start()
        edge_copies.append(copy)

    r_high, r_low = two_parts(rtwo[...])
    for g in range(SLOTS):
        for x in range(2):
            for p0, size in ((0, 8), (8, 7)):
                rows = pl.ds(g * PTS + p0, size)
                block = full[x, rows, 0:channels, :].reshape(size * channels, width_two)
                acc[x, rows] = (mm(block, r_high) + mm(block, r_low)).reshape(size, channels, width_two)
    m_high, m_low = channel_parts(table, angular, me_chan, channels, 4)
    first_l, second_l, mono = own_columns(table, angular, me_chan, channels)

    for copy in count_copies:
        copy.wait()
    offset = jnp.zeros((1, 1), jnp.int32)
    for k in range(1, n_rad):
        offset = offset + jnp.where(k <= me_rad, counts[k, 0:1, 0:1], 0)
    element = cols_of(widths.shape)
    all_widths = widths[...]

    def width_at(index):
        found = jnp.sum(jnp.where(element == index, all_widths, 0.0), axis=1, keepdims=True)
        return jnp.where(found > 0.0, found, 1.0)

    r_two = inner_radius + radial_step * cols_of((1, width_two)).astype(jnp.float32)
    inv_two = 1.0 / r_two
    base = second_l * (inv_two * inv_two) - charge * inv_two
    point = rows_of((16, 1))
    fractions = jnp.zeros((16, 1), jnp.float32)
    for p in range(1, 16):
        fractions = jnp.where(point == p, 0.5 * (1.0 - math.cos(math.pi * p / PTS)), fractions)

    for copy in edge_copies:
        copy.wait()
    inv_below = 1.0 / width_at(offset - 1)
    inv_below = jnp.where(me_rad > 0, inv_below * inv_below, 0.0)
    corner = kin_s[PTS, PTS]
    above = [jnp.where(me_rad < n_rad - 1, next_in[x].astype(jnp.float32), 0.0) for x in range(2)]
    inv_first = 1.0 / width_at(offset)
    inv_first = inv_first * inv_first
    for g in range(SLOTS):
        slot_width = width_at(offset + g)
        inv_w2 = 1.0 / slot_width
        inv_w2 = inv_w2 * inv_w2
        start = jnp.sum(jnp.where(element < offset + g, all_widths, 0.0), axis=1, keepdims=True)
        r_one = inner_radius + start + slot_width * fractions
        inv_one = 1.0 / r_one
        inv_far = 1.0 / jnp.maximum(r_one, r_two)
        weight = jnp.minimum(r_one, r_two) * inv_far * inv_far
        live = own_count > g
        for x in range(2):
            field_copies[x, g].wait()
            if g == 0:
                after = jnp.where(two_slots, full[x, PTS, 0:channels, :].astype(jnp.float32), above[x])
            else:
                after = above[x]
            after = after * inv_w2
            for p0, size in ((0, 4), (4, 4), (8, 4), (12, 3)):
                block = full[x, pl.ds(g * PTS + p0, size)].reshape(size * 2 * channels, width_two)
                used = (slice(0, size * channels), slice(0, size * 2 * channels))
                mix = mm(m_high[used], block) + mm(m_low[used], block)
                for i in range(size):
                    q = p0 + i
                    row = g * PTS + q
                    mine_q = full[x, row, 0:channels, :].astype(jnp.float32)
                    potential = base + mono * inv_far[q:q + 1, :] + (
                        first_l * (inv_one[q:q + 1] * inv_one[q:q + 1]) - charge * inv_one[q:q + 1])
                    total = acc[x, row] + kin[x, g, q] * inv_w2 + kin_s[q, PTS] * after
                    total = total + potential * mine_q
                    total = total + weight[q:q + 1, :] * mix[i * channels:(i + 1) * channels]
                    if q == 0:
                        if g == 0:
                            total = total + (below[x].astype(jnp.float32) + corner * mine_q) * inv_below
                        else:
                            total = total + (kin[x, 0, PTS] + corner * mine_q) * inv_first
                    step = time_step if x == 1 else -time_step
                    result = full[1 - x, row, 0:channels, :].astype(jnp.float32) + step * total
                    result = jnp.where(live, result, 0.0)
                    for tile in range(lane_tiles):
                        out[place(1 - x, row, tile), :] = result[:, tile * 128:(tile + 1) * 128]


def per_device(n_rad, wave, tile_elems, element_width, element_kinetic, radial_two, angular, channel_table):
    channels, _, rows, width_two = wave.shape
    tiles = width_two // 128
    raw = wave.reshape(channels, 2, rows, tiles, 128).transpose(0, 2, 3, 1, 4).reshape(-1, 128)
    vmem = pl.BlockSpec(memory_space=pltpu.VMEM)
    smem = pl.BlockSpec(memory_space=pltpu.SMEM)
    edge = pltpu.VMEM((2, channels, width_two), jnp.bfloat16)
    evolved = pl.pallas_call(
        functools.partial(kernel, n_rad),
        out_shape=jax.ShapeDtypeStruct(raw.shape, jnp.float32),
        in_specs=[vmem, smem, vmem, smem, vmem, vmem, vmem, vmem],
        out_specs=vmem,
        scratch_shapes=[
            pltpu.VMEM((2, rows, 2 * channels, width_two), jnp.bfloat16),
            edge, edge, edge,
            pltpu.VMEM((8, 128), jnp.int32),
            pltpu.VMEM((n_rad, 8, 128), jnp.int32),
            pltpu.VMEM((2, SLOTS, 16, channels, width_two), jnp.float32),
            pltpu.VMEM((2, rows, channels, width_two), jnp.float32),
            pltpu.SemaphoreType.DMA((2, SLOTS)),
            pltpu.SemaphoreType.DMA((2, SLOTS)),
            pltpu.SemaphoreType.DMA((n_rad,)),
            pltpu.SemaphoreType.DMA((n_rad,)),
            pltpu.SemaphoreType.DMA((4,)),
            pltpu.SemaphoreType.DMA((4,)),
        ],
        compiler_params=pltpu.CompilerParams(
            collective_id=0, has_side_effects=True, vmem_limit_bytes=44 * 1024 * 1024),
        cost_estimate=pl.CostEstimate(flops=6_000_000_000, bytes_accessed=10_000_000, transcendentals=0),
    )(raw, tile_elems, element_width[None, :], element_kinetic, element_kinetic, radial_two, angular,
      channel_table.T)
    evolved = evolved.reshape(channels, rows, tiles, 2, 128).transpose(0, 3, 1, 2, 4)
    return evolved.reshape(wave.shape)


def solution(mesh):
    in_specs = (P("chan", None, "rad", "grp"), P(("grp", "rad")), P("grp"), P(), P(), P(), P())
    out_specs = P("chan", None, "rad", "grp")
    return jax.shard_map(
        functools.partial(per_device, mesh.shape["rad"]), mesh=mesh, in_specs=in_specs,
        out_specs=out_specs, check_vma=False)
```

time: 28.1 us -> 24.7 us (0.88)
  local copies, waits for them, and re-layouts: 9.55 us -> 7.56 us
  other arithmetic: 1.02 us -> 0 us
  Pallas kernels: 16.5 us -> 16.2 us
    unnamed x5 -> x13, local copies, waits for them, and re-layouts: 2.01 us -> 7.56 us
    transpose x1 -> x0, local copies, waits for them, and re-layouts: 4.96 us -> none  [per_device(): return moved.transpose(2, 0, 1, 3)]
    dynamic_slice x4 -> x0, local copies, waits for them, and re-layouts: 0.98 us -> none  [the longest x1 0.76 us: per_device(): lax.dynamic_slice_in_dim(channel_table, (1 - me) * channels, channels, 0)]
    mul x2 -> x0, other arithmetic: 0.8 us -> none  [the longest x1 0.75 us: per_device(): centri = 0.5 * orbital * (orbital + 1.0)]
    slice x1 -> x0, local copies, waits for them, and re-layouts: 0.78 us -> none  [per_device(): angular[0]]
    broadcast_in_dim x3 -> x0, local copies, waits for them, and re-layouts: 0.73 us -> none  [the longest x1 0.66 us: per_device(): widths = jnp.pad(element_width, (0, lanes - total))[None, :]]
    pallas_call x1, Pallas kernels: 16.5 us -> 16.2 us  [per_device(): pl.pallas_call(functools.partial(kernel, n_rad), out_shape=jax.ShapeDtype...]
where the time goes in v2:
time: 24.7 us; the launch traced here: 24.4 us
  Pallas kernels  16.2 us (66%)
  local copies, waits for them, and re-layouts  7.56 us (31%)
  between operations  0.67 us (3%)
    pallas_call x1, Pallas kernels, per_device(): pl.pallas_call(functools.partial(kernel, n_rad), out_shape=jax.ShapeDtype...  16.2 us
    unnamed x13, local copies, waits for them, and re-layouts  7.56 us

profile of v2, /device:TPU:0, one launch (start us, length us, event | category | flops | bytes accessed | tf_op | source)
XLA Modules:
  0.0 24.4 jit_solution(11588308882087821502)
XLA Ops:
  0.7 0.0 copy-start
  0.7 1.5 %copy-done = bf16[32,2,30,512]{3,1,2,0:T(2,128)(2,1)S(1)} copy-done((bf16[32,2,30,512]{3,1,2,0:T(2,128)(2,1)S(1)}, bf16[32,2,30,512]{3,1,2,0:T(2,128)(2,1)}, u32[]{:S(2)}) %copy-start) | copy-done | bytes 1966104
  2.2 0.0 copy-start.1
  2.2 1.2 %copy-done.1 = f32[512,512]{1,0:T(8,128)S(1)} copy-done((f32[512,512]{1,0:T(8,128)S(1)}, f32[512,512]{1,0:T(8,128)}, u32[]{:S(2)}) %copy-start.1) | copy-done | bytes 1048600
  3.4 0.0 copy-start.2
  3.4 0.8 %copy-done.2 = f32[2,64,64]{2,1,0:T(8,128)S(1)} copy-done((f32[2,64,64]{2,1,0:T(8,128)S(1)}, f32[2,64,64]{2,1,0:T(8,128)}, u32[]{:S(2)}) %copy-start.2) | copy-done | bytes 32792
  4.3 0.0 copy-start.3
  4.3 0.7 %copy-done.3 = f32[16,16]{1,0:T(8,128)S(1)} copy-done((f32[16,16]{1,0:T(8,128)S(1)}, f32[16,16]{1,0:T(8,128)}, u32[]{:S(2)}) %copy-start.3) | copy-done | bytes 1048
  5.0 0.0 copy-start.4
  5.0 0.7 %copy-done.4 = s32[64,2]{0,1:T(2,128)S(1)} copy-done((s32[64,2]{0,1:T(2,128)S(1)}, s32[64,2]{0,1:T(2,128)}, u32[]{:S(2)}) %copy-start.4) | copy-done | bytes 536
  5.6 0.0 copy-start.5
  5.6 0.7 %copy-done.5 = f32[12]{0:T(128)S(1)} copy-done((f32[12]{0:T(128)S(1)}, f32[12]{0:T(128)}, u32[]{:S(2)}) %copy-start.5) | copy-done | bytes 72
  6.3 16.2 %shard_map.73 = f32[7680,128]{1,0:T(8,128)S(1)} custom-call(bf16[7680,128]{1,0:T(8,128)(2,1)S(1)} %bitcast.13, s32[1]{0:T(128)S(6)} %copy.11.tile_elems, f32[1,12]{1,0:T(1,128)S(1)} %bitcast.15, f32[16,16]{1,0:T(8,128)S(1)} %copy-done.3, f32[16,16]{1,0:T(8,128)S(1)} %copy-done.3, f32[512,512]{1,0:T(8,128)S(1)} %copy-done.1, f32[2,64,64]{2,1,0:T(8,128)S(1)} %copy-done.2, ...), custom_call_target="tpu_custom_call" | custom-call | flops 6000000000 | bytes 10000000 | tf_op jit(solution)/shard_map/pallas_call | solution.py:257
  22.5 1.9 %copy.12 = f32[32,2,30,512]{3,1,2,0:T(2,128)} copy(f32[32,2,30,512]{3,1,2,0:T(2,128)S(1)} %bitcast.12) | data formatting | bytes 7864320
Async XLA Ops:
  0.7 1.5 %copy-start = (bf16[32,2,30,512]{3,1,2,0:T(2,128)(2,1)S(1)}, bf16[32,2,30,512]{3,1,2,0:T(2,128)(2,1)}, u32[]{:S(2)}) copy-start(bf16[32,2,30,512]{3,1,2,0:T(2,128)(2,1)} %param.7) | copy-start | bytes 5898244
  2.2 1.2 %copy-start.1 = (f32[512,512]{1,0:T(8,128)S(1)}, f32[512,512]{1,0:T(8,128)}, u32[]{:S(2)}) copy-start(f32[512,512]{1,0:T(8,128)} %rtwo.1) | copy-start | bytes 3145732
  3.4 0.8 %copy-start.2 = (f32[2,64,64]{2,1,0:T(8,128)S(1)}, f32[2,64,64]{2,1,0:T(8,128)}, u32[]{:S(2)}) copy-start(f32[2,64,64]{2,1,0:T(8,128)} %angular.1) | copy-start | bytes 98308
  4.3 0.7 %copy-start.3 = (f32[16,16]{1,0:T(8,128)S(1)}, f32[16,16]{1,0:T(8,128)}, u32[]{:S(2)}) copy-start(f32[16,16]{1,0:T(8,128)} %kin_v.1) | copy-start | bytes 3076
  5.0 0.7 %copy-start.4 = (s32[64,2]{0,1:T(2,128)S(1)}, s32[64,2]{0,1:T(2,128)}, u32[]{:S(2)}) copy-start(s32[64,2]{0,1:T(2,128)} %param.13) | copy-start | bytes 1540
  5.6 0.7 %copy-start.5 = (f32[12]{0:T(128)S(1)}, f32[12]{0:T(128)}, u32[]{:S(2)}) copy-start(f32[12]{0:T(128)} %param.9) | copy-start | bytes 148

commit v3 on v2

--- a/solution.py
+++ b/solution.py
@@ -10,6 +10,7 @@
 
 PTS = 15
 SLOTS = 2
+RAW_HEAD = 128
 MESH = pl.DeviceIdType.MESH
 highest = lax.Precision.HIGHEST
 charge = 2.0
@@ -88,8 +89,8 @@
 
 
 def kernel(
-    n_rad, raw, tile_elems, widths, kin_s, kin_v, rtwo, angular, table, out,
-    full, next_in, below, spill, count, counts, kin, acc,
+    n_rad, raw_hbm, tile_elems, widths_hbm, kin_hbm, rtwo_hbm, angular_hbm, table_hbm, out_hbm,
+    out, o_sem, raw, widths, kin_v, rtwo, angular, table, l_sem, full, next_in, below, spill, count, counts, kin, acc,
     c_send, c_recv, k_send, k_recv, e_send, e_recv,
 ):
     local_rows, channels, width_two = acc.shape[1:]
@@ -103,14 +104,24 @@
     def place(x, row, tile):
         return pl.ds((row * lane_tiles + tile) * 2 + x, channels, stride=pitch)
 
+    loads = []
+    for source, target in (
+        (raw_hbm.at[:, pl.ds(0, RAW_HEAD)], raw.at[:, pl.ds(0, RAW_HEAD)]),
+        (raw_hbm.at[:, pl.ds(RAW_HEAD, pitch - RAW_HEAD)], raw.at[:, pl.ds(RAW_HEAD, pitch - RAW_HEAD)]),
+        (kin_hbm, kin_v), (rtwo_hbm, rtwo), (angular_hbm, angular), (table_hbm, table), (widths_hbm, widths),
+    ):
+        load = pltpu.make_async_copy(source, target, l_sem.at[len(loads)])
+        load.start()
+        loads.append(load)
     barrier = pltpu.get_barrier_semaphore()
     pl.semaphore_signal(barrier, inc=1, device_id={"chan": partner}, device_id_type=MESH)
     for k in range(1, n_rad):
         pl.semaphore_signal(barrier, inc=1, device_id={"rad": rad_of[k]}, device_id_type=MESH)
     count[...] = jnp.full(count.shape, tile_elems[0], jnp.int32)
 
-    for c in range(0, channels, 4):
-        out[c * pitch:(c + 4) * pitch, :] = raw[c * pitch:(c + 4) * pitch, :].astype(jnp.float32)
+    def widen(begin, end):
+        for c in range(channels):
+            out[c * pitch + begin:c * pitch + end, :] = raw[c, begin:end, :].astype(jnp.float32)
 
     def unpack(g):
         for row in range(g * PTS, (g + 1) * PTS):
@@ -119,6 +130,8 @@
                     full[x, row, 0:channels, tile * 128:(tile + 1) * 128] = out[
                         place(x, row, tile), :].astype(jnp.bfloat16)
 
+    loads[0].wait()
+    widen(0, RAW_HEAD)
     unpack(0)
     pl.semaphore_wait(barrier, n_rad)
     count_copies = []
@@ -138,6 +151,8 @@
     field_copies = {}
     for g in range(SLOTS):
         if g > 0:
+            loads[1].wait()
+            widen(RAW_HEAD, pitch)
             unpack(g)
         for x in range(2):
             copy = pltpu.make_async_remote_copy(
@@ -148,6 +163,7 @@
             copy.start()
             field_copies[x, g] = copy
 
+    loads[2].wait()
     k_high, k_low = kinetic_parts(kin_v[...])
     k_high, k_low = k_high[:, :PTS * 16], k_low[:, :PTS * 16]
     for g in range(SLOTS):
@@ -167,6 +183,7 @@
         copy.start()
         edge_copies.append(copy)
 
+    loads[3].wait()
     r_high, r_low = two_parts(rtwo[...])
     for g in range(SLOTS):
         for x in range(2):
@@ -174,6 +191,8 @@
                 rows = pl.ds(g * PTS + p0, size)
                 block = full[x, rows, 0:channels, :].reshape(size * channels, width_two)
                 acc[x, rows] = (mm(block, r_high) + mm(block, r_low)).reshape(size, channels, width_two)
+    for load in loads[4:]:
+        load.wait()
     m_high, m_low = channel_parts(table, angular, me_chan, channels, 4)
     first_l, second_l, mono = own_columns(table, angular, me_chan, channels)
 
@@ -201,10 +220,11 @@
         copy.wait()
     inv_below = 1.0 / width_at(offset - 1)
     inv_below = jnp.where(me_rad > 0, inv_below * inv_below, 0.0)
-    corner = kin_s[PTS, PTS]
+    corner = kin_v[PTS:PTS + 1, PTS:PTS + 1]
     above = [jnp.where(me_rad < n_rad - 1, next_in[x].astype(jnp.float32), 0.0) for x in range(2)]
     inv_first = 1.0 / width_at(offset)
     inv_first = inv_first * inv_first
+    stores = []
     for g in range(SLOTS):
         slot_width = width_at(offset + g)
         inv_w2 = 1.0 / slot_width
@@ -215,16 +235,18 @@
         inv_far = 1.0 / jnp.maximum(r_one, r_two)
         weight = jnp.minimum(r_one, r_two) * inv_far * inv_far
         live = own_count > g
+        after = []
         for x in range(2):
             field_copies[x, g].wait()
             if g == 0:
-                after = jnp.where(two_slots, full[x, PTS, 0:channels, :].astype(jnp.float32), above[x])
+                row = jnp.where(two_slots, full[x, PTS, 0:channels, :].astype(jnp.float32), above[x])
             else:
-                after = above[x]
-            after = after * inv_w2
-            for p0, size in ((0, 4), (4, 4), (8, 4), (12, 3)):
+                row = above[x]
+            after.append(row * inv_w2)
+        for part, (p0, size) in enumerate(((0, 4), (4, 4), (8, 4), (12, 3))):
+            used = (slice(0, size * channels), slice(0, size * 2 * channels))
+            for x in range(2):
                 block = full[x, pl.ds(g * PTS + p0, size)].reshape(size * 2 * channels, width_two)
-                used = (slice(0, size * channels), slice(0, size * 2 * channels))
                 mix = mm(m_high[used], block) + mm(m_low[used], block)
                 for i in range(size):
                     q = p0 + i
@@ -232,7 +254,7 @@
                     mine_q = full[x, row, 0:channels, :].astype(jnp.float32)
                     potential = base + mono * inv_far[q:q + 1, :] + (
                         first_l * (inv_one[q:q + 1] * inv_one[q:q + 1]) - charge * inv_one[q:q + 1])
-                    total = acc[x, row] + kin[x, g, q] * inv_w2 + kin_s[q, PTS] * after
+                    total = acc[x, row] + kin[x, g, q] * inv_w2 + kin_v[q:q + 1, PTS:PTS + 1] * after[x]
                     total = total + potential * mine_q
                     total = total + weight[q:q + 1, :] * mix[i * channels:(i + 1) * channels]
                     if q == 0:
@@ -245,21 +267,38 @@
                     result = jnp.where(live, result, 0.0)
                     for tile in range(lane_tiles):
                         out[place(1 - x, row, tile), :] = result[:, tile * 128:(tile + 1) * 128]
+            span = pl.ds((g * PTS + p0) * lane_tiles * 2, size * lane_tiles * 2)
+            store = pltpu.make_async_copy(
+                out.reshape(channels, pitch, 128).at[:, span], out_hbm.at[:, span], o_sem.at[g, part])
+            store.start()
+            stores.append(store)
+    for store in stores:
+        store.wait()
 
 
 def per_device(n_rad, wave, tile_elems, element_width, element_kinetic, radial_two, angular, channel_table):
     channels, _, rows, width_two = wave.shape
     tiles = width_two // 128
-    raw = wave.reshape(channels, 2, rows, tiles, 128).transpose(0, 2, 3, 1, 4).reshape(-1, 128)
-    vmem = pl.BlockSpec(memory_space=pltpu.VMEM)
+    raw = wave.reshape(channels, 2, rows, tiles, 128).transpose(0, 2, 3, 1, 4)
+    raw = raw.reshape(channels, -1, 128)
+    hbm = pl.BlockSpec(memory_space=pltpu.HBM)
     smem = pl.BlockSpec(memory_space=pltpu.SMEM)
     edge = pltpu.VMEM((2, channels, width_two), jnp.bfloat16)
     evolved = pl.pallas_call(
         functools.partial(kernel, n_rad),
         out_shape=jax.ShapeDtypeStruct(raw.shape, jnp.float32),
-        in_specs=[vmem, smem, vmem, smem, vmem, vmem, vmem, vmem],
-        out_specs=vmem,
+        in_specs=[hbm, smem, hbm, hbm, hbm, hbm, hbm],
+        out_specs=hbm,
         scratch_shapes=[
+            pltpu.VMEM((raw.shape[0] * raw.shape[1], 128), jnp.float32),
+            pltpu.SemaphoreType.DMA((SLOTS, 4)),
+            pltpu.VMEM(raw.shape, jnp.bfloat16),
+            pltpu.VMEM((1, element_width.shape[0]), jnp.float32),
+            pltpu.VMEM(element_kinetic.shape, jnp.float32),
+            pltpu.VMEM(radial_two.shape, jnp.float32),
+            pltpu.VMEM(angular.shape, jnp.float32),
+            pltpu.VMEM(channel_table.shape[::-1], jnp.int32),
+            pltpu.SemaphoreType.DMA((7,)),
             pltpu.VMEM((2, rows, 2 * channels, width_two), jnp.bfloat16),
             edge, edge, edge,
             pltpu.VMEM((8, 128), jnp.int32),
@@ -274,9 +313,9 @@
             pltpu.SemaphoreType.DMA((4,)),
         ],
         compiler_params=pltpu.CompilerParams(
-            collective_id=0, has_side_effects=True, vmem_limit_bytes=44 * 1024 * 1024),
+            collective_id=0, has_side_effects=True, vmem_limit_bytes=62 * 1024 * 1024),
         cost_estimate=pl.CostEstimate(flops=6_000_000_000, bytes_accessed=10_000_000, transcendentals=0),
-    )(raw, tile_elems, element_width[None, :], element_kinetic, element_kinetic, radial_two, angular,
+    )(raw, tile_elems, element_width[None, :], element_kinetic, radial_two, angular,
       channel_table.T)
     evolved = evolved.reshape(channels, rows, tiles, 2, 128).transpose(0, 3, 1, 2, 4)
     return evolved.reshape(wave.shape)

time: 24.7 us -> 23.7 us (0.960)
  local copies, waits for them, and re-layouts: 7.56 us -> 5.38 us
  Pallas kernels: 16.2 us -> 17.5 us
    unnamed x13 -> x1, local copies, waits for them, and re-layouts: 7.56 us -> 5.38 us
    pallas_call x1, Pallas kernels: 16.2 us -> 17.5 us  [per_device(): pl.pallas_call(functools.partial(kernel, n_rad), out_shape=jax.ShapeDtype...]
where the time goes in v3:
time: 23.7 us; the launch traced here: 23.5 us
  Pallas kernels  17.5 us (74%)
  local copies, waits for them, and re-layouts  5.38 us (23%)
  between operations  0.66 us (3%)
    pallas_call x1, Pallas kernels, per_device(): pl.pallas_call(functools.partial(kernel, n_rad), out_shape=jax.ShapeDtype...  17.5 us
    unnamed x1, local copies, waits for them, and re-layouts  5.38 us

profile of v3, /device:TPU:0, one launch (start us, length us, event | category | flops | bytes accessed | tf_op | source)
XLA Modules:
  0.0 23.5 jit_solution(18111904774862598737)
XLA Ops:
  0.7 17.5 %shard_map.73 = f32[32,240,128]{2,1,0:T(8,128)} custom-call(bf16[32,240,128]{2,1,0:T(8,128)(2,1)} %bitcast.13, s32[1]{0:T(128)S(6)} %copy.11.tile_elems, f32[1,12]{1,0:T(1,128)} %bitcast.15, f32[16,16]{1,0:T(8,128)} %kin_hbm.1, f32[512,512]{1,0:T(8,128)} %rtwo_hbm.1, f32[2,64,64]{2,1,0:T(8,128)} %angular_hbm.1, s32[2,64]{1,0:T(2,128)} %bitcast.14), custom_call_target="tpu_custom_call" | custom-call | flops 6000000000 | bytes 10000000 | tf_op jit(solution)/shard_map/pallas_call | solution.py:287
  18.1 5.4 %copy.12 = f32[32,2,30,512]{3,1,2,0:T(2,128)} copy(f32[32,2,30,512]{3,1,2,0:T(2,128)} %bitcast.12) | data formatting | bytes 7864320

commit v4 on v3

--- a/solution.py
+++ b/solution.py
@@ -89,8 +89,8 @@
 
 
 def kernel(
-    n_rad, raw_hbm, tile_elems, widths_hbm, kin_hbm, rtwo_hbm, angular_hbm, table_hbm, out_hbm,
-    out, o_sem, raw, widths, kin_v, rtwo, angular, table, l_sem, full, next_in, below, spill, count, counts, kin, acc,
+    n_rad, raw_hbm, tile_elems, widths_hbm, kin_hbm, rtwo_hbm, angular_hbm, table_hbm, out,
+    raw, widths, kin_v, rtwo, angular, table, l_sem, full, next_in, below, spill, count, counts, kin, acc,
     c_send, c_recv, k_send, k_recv, e_send, e_recv,
 ):
     local_rows, channels, width_two = acc.shape[1:]
@@ -224,7 +224,6 @@
     above = [jnp.where(me_rad < n_rad - 1, next_in[x].astype(jnp.float32), 0.0) for x in range(2)]
     inv_first = 1.0 / width_at(offset)
     inv_first = inv_first * inv_first
-    stores = []
     for g in range(SLOTS):
         slot_width = width_at(offset + g)
         inv_w2 = 1.0 / slot_width
@@ -243,7 +242,7 @@
             else:
                 row = above[x]
             after.append(row * inv_w2)
-        for part, (p0, size) in enumerate(((0, 4), (4, 4), (8, 4), (12, 3))):
+        for p0, size in ((0, 4), (4, 4), (8, 4), (12, 3)):
             used = (slice(0, size * channels), slice(0, size * 2 * channels))
             for x in range(2):
                 block = full[x, pl.ds(g * PTS + p0, size)].reshape(size * 2 * channels, width_two)
@@ -267,13 +266,6 @@
                     result = jnp.where(live, result, 0.0)
                     for tile in range(lane_tiles):
                         out[place(1 - x, row, tile), :] = result[:, tile * 128:(tile + 1) * 128]
-            span = pl.ds((g * PTS + p0) * lane_tiles * 2, size * lane_tiles * 2)
-            store = pltpu.make_async_copy(
-                out.reshape(channels, pitch, 128).at[:, span], out_hbm.at[:, span], o_sem.at[g, part])
-            store.start()
-            stores.append(store)
-    for store in stores:
-        store.wait()
 
 
 def per_device(n_rad, wave, tile_elems, element_width, element_kinetic, radial_two, angular, channel_table):
@@ -286,12 +278,10 @@
     edge = pltpu.VMEM((2, channels, width_two), jnp.bfloat16)
     evolved = pl.pallas_call(
         functools.partial(kernel, n_rad),
-        out_shape=jax.ShapeDtypeStruct(raw.shape, jnp.float32),
+        out_shape=pltpu.VMEM((raw.shape[0] * raw.shape[1], 128), jnp.float32),
         in_specs=[hbm, smem, hbm, hbm, hbm, hbm, hbm],
-        out_specs=hbm,
+        out_specs=pl.BlockSpec(memory_space=pltpu.VMEM),
         scratch_shapes=[
-            pltpu.VMEM((raw.shape[0] * raw.shape[1], 128), jnp.float32),
-            pltpu.SemaphoreType.DMA((SLOTS, 4)),
             pltpu.VMEM(raw.shape, jnp.bfloat16),
             pltpu.VMEM((1, element_width.shape[0]), jnp.float32),
             pltpu.VMEM(element_kinetic.shape, jnp.float32),
@@ -313,7 +303,7 @@
             pltpu.SemaphoreType.DMA((4,)),
         ],
         compiler_params=pltpu.CompilerParams(
-            collective_id=0, has_side_effects=True, vmem_limit_bytes=62 * 1024 * 1024),
+            collective_id=0, has_side_effects=True, vmem_limit_bytes=58 * 1024 * 1024),
         cost_estimate=pl.CostEstimate(flops=6_000_000_000, bytes_accessed=10_000_000, transcendentals=0),
     )(raw, tile_elems, element_width[None, :], element_kinetic, radial_two, angular,
       channel_table.T)

time: 23.7 us -> 19.3 us (0.81)
  local copies, waits for them, and re-layouts: 5.38 us -> 1.93 us
  Pallas kernels: 17.5 us -> 16.6 us
    unnamed x1, local copies, waits for them, and re-layouts: 5.38 us -> 1.93 us
    pallas_call x1, Pallas kernels: 17.5 us -> 16.6 us  [per_device(): pl.pallas_call(functools.partial(kernel, n_rad), out_shape=pltpu.VMEM((ra...]
where the time goes in v4:
time: 19.3 us; the launch traced here: 19.2 us
  Pallas kernels  16.6 us (86%)
  local copies, waits for them, and re-layouts  1.93 us (10%)
  between operations  0.66 us (3%)
    pallas_call x1, Pallas kernels, per_device(): pl.pallas_call(functools.partial(kernel, n_rad), out_shape=pltpu.VMEM((ra...  16.6 us
    unnamed x1, local copies, waits for them, and re-layouts  1.93 us

profile of v4, /device:TPU:0, one launch (start us, length us, event | category | flops | bytes accessed | tf_op | source)
XLA Modules:
  0.0 19.2 jit_solution(8017382775108093614)
XLA Ops:
  0.7 16.6 %shard_map.73 = f32[7680,128]{1,0:T(8,128)S(1)} custom-call(bf16[32,240,128]{2,1,0:T(8,128)(2,1)} %bitcast.13, s32[1]{0:T(128)S(6)} %copy.12.tile_elems, f32[1,12]{1,0:T(1,128)} %bitcast.15, f32[16,16]{1,0:T(8,128)} %kin_hbm.1, f32[512,512]{1,0:T(8,128)} %rtwo_hbm.1, f32[2,64,64]{2,1,0:T(8,128)} %angular_hbm.1, s32[2,64]{1,0:T(2,128)} %bitcast.14), custom_call_target="tpu_custom_call" | custom-call | flops 6000000000 | bytes 10000000 | tf_op jit(solution)/shard_map/pallas_call | solution.py:279
  17.3 1.9 %copy.11 = f32[32,2,30,512]{3,1,2,0:T(2,128)} copy(f32[32,2,30,512]{3,1,2,0:T(2,128)S(1)} %bitcast.12) | data formatting | bytes 7864320

commit v5 on v4

--- a/solution.py
+++ b/solution.py
@@ -104,15 +104,13 @@
     def place(x, row, tile):
         return pl.ds((row * lane_tiles + tile) * 2 + x, channels, stride=pitch)
 
-    loads = []
-    for source, target in (
+    tail = pitch - RAW_HEAD
+    loads = [pltpu.make_async_copy(source, target, l_sem.at[i]) for i, (source, target) in enumerate((
         (raw_hbm.at[:, pl.ds(0, RAW_HEAD)], raw.at[:, pl.ds(0, RAW_HEAD)]),
-        (raw_hbm.at[:, pl.ds(RAW_HEAD, pitch - RAW_HEAD)], raw.at[:, pl.ds(RAW_HEAD, pitch - RAW_HEAD)]),
-        (kin_hbm, kin_v), (rtwo_hbm, rtwo), (angular_hbm, angular), (table_hbm, table), (widths_hbm, widths),
-    ):
-        load = pltpu.make_async_copy(source, target, l_sem.at[len(loads)])
-        load.start()
-        loads.append(load)
+        (raw_hbm.at[:, pl.ds(RAW_HEAD, tail)], raw.at[:, pl.ds(RAW_HEAD, tail)]),
+        (kin_hbm, kin_v), (rtwo_hbm, rtwo), (angular_hbm, angular), (table_hbm, table), (widths_hbm, widths)))]
+    for i in (2, 4, 5, 6, 0, 1, 3):
+        loads[i].start()
     barrier = pltpu.get_barrier_semaphore()
     pl.semaphore_signal(barrier, inc=1, device_id={"chan": partner}, device_id_type=MESH)
     for k in range(1, n_rad):
@@ -130,6 +128,13 @@
                     full[x, row, 0:channels, tile * 128:(tile + 1) * 128] = out[
                         place(x, row, tile), :].astype(jnp.bfloat16)
 
+    loads[2].wait()
+    k_high, k_low = kinetic_parts(kin_v[...])
+    k_high, k_low = k_high[:, :PTS * 16], k_low[:, :PTS * 16]
+    for load in loads[4:]:
+        load.wait()
+    m_high, m_low = channel_parts(table, angular, me_chan, channels, 4)
+    first_l, second_l, mono = own_columns(table, angular, me_chan, channels)
     loads[0].wait()
     widen(0, RAW_HEAD)
     unpack(0)
@@ -163,9 +168,6 @@
             copy.start()
             field_copies[x, g] = copy
 
-    loads[2].wait()
-    k_high, k_low = kinetic_parts(kin_v[...])
-    k_high, k_low = k_high[:, :PTS * 16], k_low[:, :PTS * 16]
     for g in range(SLOTS):
         for x in range(2):
             for cb in range(channels // 16):
@@ -191,10 +193,6 @@
                 rows = pl.ds(g * PTS + p0, size)
                 block = full[x, rows, 0:channels, :].reshape(size * channels, width_two)
                 acc[x, rows] = (mm(block, r_high) + mm(block, r_low)).reshape(size, channels, width_two)
-    for load in loads[4:]:
-        load.wait()
-    m_high, m_low = channel_parts(table, angular, me_chan, channels, 4)
-    first_l, second_l, mono = own_columns(table, angular, me_chan, channels)
 
     for copy in count_copies:
         copy.wait()

time: 19.3 us -> 19.6 us (1.016)
  Pallas kernels: 16.6 us -> 16.8 us
    pallas_call x1, Pallas kernels: 16.6 us -> 16.8 us  [per_device(): pl.pallas_call(functools.partial(kernel, n_rad), out_shape=pltpu.VMEM((ra...]
where the time goes in v5:
time: 19.6 us; the launch traced here: 19.4 us
  Pallas kernels  16.8 us (86%)
  local copies, waits for them, and re-layouts  1.93 us (10%)
  between operations  0.66 us (3%)
    pallas_call x1, Pallas kernels, per_device(): pl.pallas_call(functools.partial(kernel, n_rad), out_shape=pltpu.VMEM((ra...  16.8 us
    unnamed x1, local copies, waits for them, and re-layouts  1.93 us

profile of v5, /device:TPU:0, one launch (start us, length us, event | category | flops | bytes accessed | tf_op | source)
XLA Modules:
  0.0 19.4 jit_solution(9487119199227143283)
XLA Ops:
  0.7 16.8 %shard_map.73 = f32[7680,128]{1,0:T(8,128)S(1)} custom-call(bf16[32,240,128]{2,1,0:T(8,128)(2,1)} %bitcast.13, s32[1]{0:T(128)S(6)} %copy.12.tile_elems, f32[1,12]{1,0:T(1,128)} %bitcast.15, f32[16,16]{1,0:T(8,128)} %kin_hbm.1, f32[512,512]{1,0:T(8,128)} %rtwo_hbm.1, f32[2,64,64]{2,1,0:T(8,128)} %angular_hbm.1, s32[2,64]{1,0:T(2,128)} %bitcast.14), custom_call_target="tpu_custom_call" | custom-call | flops 6000000000 | bytes 10000000 | tf_op jit(solution)/shard_map/pallas_call | solution.py:277
  17.5 1.9 %copy.11 = f32[32,2,30,512]{3,1,2,0:T(2,128)} copy(f32[32,2,30,512]{3,1,2,0:T(2,128)S(1)} %bitcast.12) | data formatting | bytes 7864320
